TPU v7x, 512 devices: a whole 4x4x16 slice. The times are simulated.
512 devices in a mesh: patch: 32 (over y_lo, z), head: 8 (over y_hi, x), cfg: 2 (over core).
Axes of the slice: x: 4, y: 4 (y_hi: 2, y_lo: 2; y = y_hi * 2 + y_lo), z: 16, core: 2. Of those that a mesh axis runs over, the one named last changes fastest.
Arguments:
- qkv: bfloat16 [2, 3, 8192, 3072], P('cfg', None, ('patch', 'head')), may hold values from -45 to 45
- stale_kv: bfloat16 [2, 2, 8192, 3072], P('cfg', None, 'patch', 'head'), may hold values from -10 to 10
- tokens_in: bfloat16 [8192, 3072], P(('patch', 'head'), 'cfg'), may hold values from -6 to 6
- out_weight: bfloat16 [3072, 3072], P('head'), may hold values from -0.109375 to 0.109375
- gate: float32 [3072], P('cfg'), may hold values from 0.1 to 1.9
Outputs:
- next_kv: bfloat16 [2, 2, 8192, 3072], P('cfg', None, 'patch', 'head')
- guided: bfloat16 [8192, 3072], P(('patch', 'head'), 'cfg')
All inputs are finite; a program needn't handle non-finite values.
Results may differ from a plain program's by a relative error of at most 0.019.
Values may be sent and summed in bfloat16 or wider, within the bound.
A program may use at most 64 MiB of HBM per device.

v0:
```python
import jax
import jax.numpy as jnp
from jax import lax
from jax.sharding import PartitionSpec as P

HD = 128


guide_scale = 6.0


def swapped(value, axis, distance):
    mask = 2**distance
    pairs = [(source, source ^ mask) for source in range(lax.axis_size(axis))]
    return lax.ppermute(value, axis, pairs)


def body(qkv, stale_kv, tokens_in, out_weight, gate):
    gathered_heads = lax.all_to_all(qkv, "head", split_axis=3, concat_axis=2, tiled=True)
    rows = gathered_heads.shape[2]
    width = gathered_heads.shape[3]
    count = width // HD
    scale = HD ** (-0.5)
    queries = gathered_heads[0, 0].reshape(rows, count, HD)
    fresh_keys = gathered_heads[0, 1].reshape(rows, count, HD)
    fresh_values = gathered_heads[0, 2].reshape(rows, count, HD)
    next_kv = gathered_heads[:, 1:3]
    own_scores = (
        jnp.einsum("qhd,khd->hqk", queries, fresh_keys, preferred_element_type=jnp.float32) * scale
    )
    own_max = jnp.max(own_scores, axis=-1)
    own_weights = jnp.exp(own_scores - own_max[..., None])
    own_totals = jnp.sum(own_weights, axis=-1)
    own_summed = jnp.einsum(
        "hqk,khd->hqd",
        own_weights.astype(jnp.bfloat16),
        fresh_values,
        preferred_element_type=jnp.float32,
    )
    own_start = lax.axis_index("patch") * rows
    initial = (own_max, own_totals, own_summed)
    keys_piece = lax.all_gather(stale_kv[0, 0], "patch", axis=0, tiled=True)
    values_piece = lax.all_gather(stale_kv[0, 1], "patch", axis=0, tiled=True)
    length = keys_piece.shape[0]
    block = 512
    blocks = length // block
    keys_blocks = keys_piece.reshape(blocks, block, count, HD)
    values_blocks = values_piece.reshape(blocks, block, count, HD)
    offsets = jnp.arange(blocks, dtype=jnp.int32) * block

    def one_block(state, inputs):
        maxima, totals, summed = state
        key_block, value_block, offset = inputs
        block_scores = (
            jnp.einsum("qhd,khd->hqk", queries, key_block, preferred_element_type=jnp.float32)
            * scale
        )
        position = offset + jnp.arange(block, dtype=jnp.int32)
        inside = (position >= own_start) & (position < own_start + rows)
        block_scores = jnp.where(inside[None, None, :], -jnp.inf, block_scores)
        new_max = jnp.maximum(maxima, jnp.max(block_scores, axis=-1))
        factor = jnp.exp(maxima - new_max)
        block_weights = jnp.exp(block_scores - new_max[..., None])
        totals = totals * factor + jnp.sum(block_weights, axis=-1)
        summed = summed * factor[..., None] + jnp.einsum(
            "hqk,khd->hqd",
            block_weights.astype(jnp.bfloat16),
            value_block,
            preferred_element_type=jnp.float32,
        )
        return ((new_max, totals, summed), None)

    state, ignored = lax.scan(one_block, initial, (keys_blocks, values_blocks, offsets))
    maxima, totals, summed = state
    attended = (summed / totals[..., None]).astype(jnp.bfloat16)
    weight_heads = out_weight.reshape(count, HD, out_weight.shape[1])
    partial_terms = jnp.einsum(
        "hqd,hde->qe", attended, weight_heads, preferred_element_type=jnp.float32
    )
    branch_index = lax.axis_index("cfg")
    full_width = partial_terms.shape[1]
    half_width = full_width // 2
    own_sums = lax.psum_scatter(
        partial_terms.astype(jnp.bfloat16), "head", scatter_dimension=0, tiled=True
    ).astype(jnp.float32)
    kept_half = lax.dynamic_slice_in_dim(own_sums, branch_index * half_width, half_width, 1)
    sending = lax.dynamic_slice_in_dim(own_sums, (1 - branch_index) * half_width, half_width, 1)
    other_half = swapped(sending.astype(jnp.bfloat16), "cfg", 0).astype(sending.dtype)
    conditioned = jnp.where(branch_index == 0, kept_half, other_half)
    unconditioned = jnp.where(branch_index == 0, other_half, kept_half)
    mixed = guide_scale * conditioned - (guide_scale - 1.0) * unconditioned
    guided = (tokens_in.astype(jnp.float32) + gate * mixed).astype(jnp.bfloat16)
    return (next_kv, guided)


def solution(mesh):
    in_specs = (
        P("cfg", None, ("patch", "head"), None),
        P("cfg", None, "patch", "head"),
        P(("patch", "head"), "cfg"),
        P("head", None),
        P("cfg"),
    )
    out_specs = (P("cfg", None, "patch", "head"), P(("patch", "head"), "cfg"))
    return jax.shard_map(body, mesh=mesh, in_specs=in_specs, out_specs=out_specs, check_vma=False)
```

profile of v0, /device:TPU:1, one launch (start us, length us, event | category | flops | bytes accessed | tf_op | source)
XLA Modules:
  0.0 495.6 jit_solution(726804826778598199)
XLA Ops:
  7.2 1.9 fusion.28
  9.9 4.7 copy.50
  14.7 6.6 %reshape.35 = bf16[8,2,18432]{2,1,0:T(2,128)(2,1)} reshape(bf16[3072,1,3,32]{3,2,1,0:T(4,128)(2,1)} %bitcast.59) | data formatting | bytes 1179648
  21.3 7.5 %all-to-all-start = ((bf16[8,2,18432]{2,1,0:T(2,128)(2,1)}), bf16[8,2,18432]{2,1,0:T(2,128)(2,1)S(1)}, u32[]{:S(2)}, u32[]{:S(2)}) async-start(bf16[8,2,18432]{2,1,0:T(2,128)(2,1)} %reshape.35), calls=%async_computation | async-start | bytes 1179648 | tf_op jit(solution)/shard_map/all_to_all | solution.py:19
  28.8 9.6 %all-to-all-done = bf16[8,2,18432]{2,1,0:T(2,128)(2,1)S(1)} async-done(((bf16[8,2,18432]{2,1,0:T(2,128)(2,1)}), bf16[8,2,18432]{2,1,0:T(2,128)(2,1)S(1)}, u32[]{:S(2)}, u32[]{:S(2)}) %all-to-all-start) | async-done | bytes 589856 | tf_op jit(solution)/shard_map/all_to_all | solution.py:19
  38.4 4.2 reshape.36
  42.6 4.2 copy.71
  49.8 91.8 %all-gather.5.cloned.1.call-done = bf16[1,1,8192,384]{3,2,1,0:T(8,128)(2,1)} async-done(((bf16[1,1,256,384]{3,2,1,0:T(8,128)(2,1)}), bf16[1,1,8192,384]{3,2,1,0:T(8,128)(2,1)}) %all-gather.5.cloned.1.call-update) | async-done | bytes 6291472 | tf_op jit(solution)/shard_map/all_gather | solution.py:42
  141.7 16.7 %reshape.33 = bf16[16,512,3,128]{3,2,1,0:T(4,128)(2,1)} reshape(bf16[1,1,8192,384]{3,2,1,0:T(8,128)(2,1)} %all-gather.5.cloned.1.call-done) | data formatting | bytes 12582912 | tf_op jit(solution)/shard_map/reshape | solution.py:47
  158.3 7.7 %copy.62 = bf16[16,512,3,128]{3,1,2,0:T(8,128)(2,1)} copy(bf16[16,512,3,128]{3,2,1,0:T(4,128)(2,1)} %reshape.33) | data formatting | bytes 12582912 | tf_op jit(solution)/shard_map/while | solution.py:73
  166.1 115.1 %all-gather.7.cloned.1.call-done = bf16[1,1,8192,384]{3,2,1,0:T(8,128)(2,1)} async-done(((bf16[1,1,256,384]{3,2,1,0:T(8,128)(2,1)}), bf16[1,1,8192,384]{3,2,1,0:T(8,128)(2,1)}) %all-gather.7.cloned.1.call-update) | async-done | bytes 6291472 | tf_op jit(solution)/shard_map/all_gather | solution.py:43
  281.1 16.7 %reshape.34 = bf16[16,512,3,128]{3,2,1,0:T(4,128)(2,1)} reshape(bf16[1,1,8192,384]{3,2,1,0:T(8,128)(2,1)} %all-gather.7.cloned.1.call-done) | data formatting | bytes 12582912 | tf_op jit(solution)/shard_map/reshape | solution.py:48
  297.8 7.8 %copy.64 = bf16[16,512,3,128]{3,1,2,0:T(8,128)(2,1)} copy(bf16[16,512,3,128]{3,2,1,0:T(4,128)(2,1)} %reshape.34) | data formatting | bytes 12582912 | tf_op jit(solution)/shard_map/while | solution.py:73
  305.6 71.4 %while.15 = (s32[]{:T(128)}, f32[3,256]{1,0:T(4,128)S(1)}, f32[3,256]{1,0:T(4,128)S(1)}, f32[3,256,128]{2,1,0:T(8,128)S(1)}, s32[16]{0:T(128)S(1)}, /*index=5*/s...) while((s32[]{:T(128)}, f32[3,256]{1,0:T(4,128)S(1)}, ...), condition=%wide.region_5.6_spmd, body=%wide.region_2.5_spmd.sunk | while | flops 204279296 | bytes 6538389 | solution.py:73
  308.5 1.5 convolution_add_fusion.2
  313.0 1.5 convolution_add_fusion.2
  317.5 1.5 convolution_add_fusion.2
  321.9 1.5 convolution_add_fusion.2
  326.4 1.5 convolution_add_fusion.2
  330.9 1.5 convolution_add_fusion.2
  335.3 1.5 convolution_add_fusion.2
  339.8 1.5 convolution_add_fusion.2
  344.2 1.5 convolution_add_fusion.2
  348.7 1.5 convolution_add_fusion.2
  353.2 1.5 convolution_add_fusion.2
  357.6 1.5 convolution_add_fusion.2
  362.1 1.5 convolution_add_fusion.2
  366.6 1.5 convolution_add_fusion.2
  377.1 2.2 fusion.14
  379.3 102.5 %reduce-scatter.2.cloned.1.call-done = bf16[32,3072]{1,0:T(8,128)(2,1)} async-done(((bf16[256,3072]{1,0:T(8,128)(2,1)}), bf16[32,3072]{1,0:T(8,128)(2,1)}) %reduce-scatter.2.cloned.1.call-update) | async-done | bytes 196624 | tf_op jit(solution)/shard_map/reduce_scatter | solution.py:83
  482.8 3.7 collective-permute-start
  487.5 1.6 fusion.24
  (139 shorter events, 55.0 us)
Async XLA Ops:
  7.2 369.9 %copy-start = (bf16[384,3072]{1,0:T(8,128)(2,1)S(1)}, bf16[384,3072]{1,0:T(8,128)(2,1)}, u32[]{:S(2)}) copy-start(bf16[384,3072]{1,0:T(8,128)(2,1)} %param.10) | copy-start | bytes 7077892
  7.2 134.5 %all-gather.5.cloned.1.call-start = ((), (), s32[]{:S(2)}) async-start(), calls=%async_computation.3 | async-start | bytes 6488064 | tf_op jit(solution)/shard_map/all_gather | solution.py:42
  9.2 271.9 %all-gather.7.cloned.1.call-start = ((), (), s32[]{:S(2)}) async-start(), calls=%async_computation.4 | async-start | bytes 6488064 | tf_op jit(solution)/shard_map/all_gather | solution.py:43
  21.3 17.1 %all-to-all-start = ((bf16[8,2,18432]{2,1,0:T(2,128)(2,1)}), bf16[8,2,18432]{2,1,0:T(2,128)(2,1)S(1)}, u32[]{:S(2)}, u32[]{:S(2)}) async-start(bf16[8,2,18432]{2,1,0:T(2,128)(2,1)} %reshape.35), calls=%async_computation | async-start | bytes 1179648 | tf_op jit(solution)/shard_map/all_to_all | solution.py:19
  28.8 453.0 %reduce-scatter.2.cloned.1.call-start = ((), (), s32[]{:S(2)}) async-start(), calls=%async_computation.2 | async-start | bytes 1769472 | tf_op jit(solution)/shard_map/reduce_scatter | solution.py:83
  379.3 108.2 %copy-start.1 = (bf16[32,1536]{1,0:T(8,128)(2,1)S(1)}, bf16[32,1536]{1,0:T(8,128)(2,1)}, u32[]{:S(2)}) copy-start(bf16[32,1536]{1,0:T(8,128)(2,1)} %param.9) | copy-start | bytes 294916
  379.3 108.2 %copy-start.2 = (f32[1536]{0:T(1024)S(1)}, f32[1536]{0:T(1024)}, u32[]{:S(2)}) copy-start(f32[1536]{0:T(1024)} %param.11) | copy-start | bytes 18436
  482.8 4.7 collective-permute-start
Sparse Core Ops, SparseCore 0:
  10.1 131.5 all-gather.4
  143.8 137.3 all-gather.6
  379.4 102.3 reduce-scatter.1
where the time goes:
time: 499 us; the launch traced here: 496 us
  waiting for transfers between devices  320 us (64%)
  local copies, waits for them, and re-layouts  82.1 us (16%)
  matrix products  50.5 us (10%)
  other arithmetic  17.1 us (3%)
  between operations  13.9 us (3%)
  starting transfers between devices  11.3 us (2%)
    all_gather x1, waiting for transfers between devices, body(): values_piece = lax.all_gather(stale_kv[0, 1], 'patch', axis=0, tiled=True)  115 us
    reduce_scatter x1, waiting for transfers between devices, body(): lax.psum_scatter(partial_terms.astype(jnp.bfloat16), 'head', scatter_dime...  102 us
    all_gather x1, waiting for transfers between devices, body(): keys_piece = lax.all_gather(stale_kv[0, 0], 'patch', axis=0, tiled=True)  91.8 us
    dot_general x16, matrix products, one_block(): jnp.einsum('hqk,khd->hqd', block_weights.astype(jnp.bfloat16), value_bloc...  24.6 us
    dot_general x16, matrix products, one_block(): jnp.einsum('qhd,khd->hqk', queries, key_block, preferred_element_type=jnp...  22.2 us
    reshape x1, local copies, waits for them, and re-layouts, body(): values_blocks = values_piece.reshape(blocks, block, count, HD)  16.7 us
    reshape x1, local copies, waits for them, and re-layouts, body(): keys_blocks = keys_piece.reshape(blocks, block, count, HD)  16.7 us
    while x3, local copies, waits for them, and re-layouts, body(): lax.scan(one_block, initial, (keys_blocks, values_blocks, offsets))  15.7 us
  transfers between devices with their start and end apart: 5, of which 5 were waited for; matrix products, arithmetic and copies ran while one was open for 10% of the time, Pallas kernels for 0%

commit v1 on v0

v1 whole, which is shorter than its diff:
```python
import functools
import math

import jax
import jax.numpy as jnp
from jax import lax
from jax.experimental import pallas as pl
from jax.experimental.pallas import tpu as pltpu
from jax.sharding import PartitionSpec as P

HD = 128
GUIDE = 6.0
MESH = pl.DeviceIdType.MESH
BF16 = jnp.bfloat16
F32 = jnp.float32
SCALE2 = HD ** (-0.5) * math.log2(math.e)


def kernel(
    nz,
    nh,
    qkv_ref,
    stale_ref,
    tokens_ref,
    weight_ref,
    gate_ref,
    next_ref,
    guided_ref,
    fresh,
    own,
    kv,
    far,
    qc,
    qpart,
    maxima,
    totals,
    summed,
    part_out,
    part_in,
    stat_out,
    stat_in,
    att,
    att_other,
    mixed,
    weight,
    tokens,
    gate,
    rs_out,
    rs_in,
    ring_send,
    ring_recv,
    a2a_send,
    a2a_recv,
    part_send,
    part_recv,
    cfg_send,
    cfg_recv,
    rs_send,
    rs_recv,
    local_sem,
):
    tok = qkv_ref.shape[2]
    rows = tok * nh
    width = stale_ref.shape[3]
    count = width // HD
    half = tokens_ref.shape[1]
    nfull = nz // 2 - 1
    patch = lax.axis_index("patch")
    head = lax.axis_index("head")
    cfg = lax.axis_index("cfg")
    column = patch // nz
    z = lax.rem(patch, nz)
    ahead = {"patch": column * nz + lax.rem(z + 1, nz)}
    behind = {"patch": column * nz + lax.rem(z + nz - 1, nz)}
    partner = {"patch": lax.rem(patch + nz, 2 * nz)}
    other = {"cfg": 1 - cfg}
    around = (ahead, behind)
    peers = [{"head": lax.rem(head + i, nh)} for i in range(1, nh)]

    def remote(src, dst, send, recv, device):
        return pltpu.make_async_remote_copy(
            src_ref=src,
            dst_ref=dst,
            send_sem=send,
            recv_sem=recv,
            device_id=device,
            device_id_type=MESH,
        )

    def ring_first(k, side):
        return remote(
            stale_ref.at[0, :, :, pl.ds(k * HD, HD)],
            kv.at[0, k, :, side],
            ring_send.at[side, 0, k],
            ring_recv.at[side, 0, k],
            around[side],
        )

    def ring_next(slot, k, side):
        return remote(
            kv.at[slot - 1, k, :, side],
            kv.at[slot, k, :, side],
            ring_send.at[side, slot, k],
            ring_recv.at[side, slot, k],
            around[side],
        )

    def ring_far(k, side):
        return remote(
            kv.at[nfull - 1, k, side, side],
            far.at[k, side],
            ring_send.at[side, nfull, k],
            ring_recv.at[side, nfull, k],
            around[side],
        )

    def arrived(slot, k, side):
        remote(
            kv.at[slot, k, :, side],
            kv.at[slot, k, :, side],
            ring_send.at[side, slot, k],
            ring_recv.at[side, slot, k],
            around[side],
        ).wait_recv()

    def a2a_to(i):
        target = lax.rem(head + i, nh)
        return remote(
            qkv_ref.at[0, :, :, pl.ds(pl.multiple_of(target * width, HD), width)],
            fresh.at[:, pl.ds(pl.multiple_of(head * tok, tok), tok)],
            a2a_send.at[i],
            a2a_recv.at[i],
            peers[i - 1],
        )

    own_copy = pltpu.make_async_copy(stale_ref.at[0], own, local_sem.at[0])
    mine_copy = pltpu.make_async_copy(
        qkv_ref.at[0, :, :, pl.ds(pl.multiple_of(head * width, HD), width)],
        fresh.at[:, pl.ds(pl.multiple_of(head * tok, tok), tok)],
        local_sem.at[1],
    )
    weight_copy = pltpu.make_async_copy(
        weight_ref.at[:, pl.ds(pl.multiple_of(cfg * half, HD), half)], weight, local_sem.at[2]
    )
    tokens_copy = pltpu.make_async_copy(tokens_ref, tokens, local_sem.at[3])
    gate_copy = pltpu.make_async_copy(gate_ref, gate, local_sem.at[4])
    next_copy = pltpu.make_async_copy(fresh.at[pl.ds(1, 2)], next_ref.at[0], local_sem.at[5])

    barrier = pltpu.get_barrier_semaphore()
    greeted = [ahead, behind, partner, other] + peers
    for device in greeted:
        pl.semaphore_signal(barrier, inc=1, device_id=device, device_id_type=MESH)
    own_copy.start()
    mine_copy.start()
    weight_copy.start()
    tokens_copy.start()
    gate_copy.start()
    pl.semaphore_wait(barrier, len(greeted))

    for k in range(count):
        for side in range(2):
            ring_first(k, side).start()
    for i in range(1, nh):
        a2a_to(i).start()

    def pass_on(slot):
        for k in range(count):
            for side in range(2):
                arrived(slot, k, side)
                if isinstance(slot, int) and slot == nfull - 1:
                    ring_far(k, side).start()
                else:
                    ring_next(slot + 1, k, side).start()

    def attend(k, start, size, keys, values, first=False):
        span = pl.ds(start, size)
        scores = lax.dot_general(
            qc[k, span], keys, (((1,), (1,)), ((), ())), preferred_element_type=F32
        )
        block_max = jnp.max(scores, axis=1, keepdims=True)
        if first:
            new_max = jnp.broadcast_to(block_max, (size, HD))
        else:
            old_max = maxima[k, span]
            new_max = jnp.maximum(old_max, block_max)
            factor = jnp.exp2((old_max - new_max) * SCALE2)
        lanes = [
            jnp.exp2((scores[:, j : j + HD] - new_max) * SCALE2)
            for j in range(0, scores.shape[1], HD)
        ]
        total = functools.reduce(jnp.add, lanes)
        weights = jnp.concatenate([lane.astype(BF16) for lane in lanes], axis=1)
        product = jnp.dot(weights, values, preferred_element_type=F32)
        maxima[k, span] = new_max
        if first:
            totals[k, span] = total
            summed[k, span] = product
        else:
            totals[k, span] = totals[k, span] * factor + total
            summed[k, span] = summed[k, span] * factor + product

    def attend_slot(slot, k):
        keys = kv[slot, k, 0].reshape(2 * rows, HD)
        values = kv[slot, k, 1].reshape(2 * rows, HD)
        for start in (0, rows):
            attend(k, start, rows, keys, values)

    early = min(2, nfull)
    pass_on(0)
    mine_copy.wait()
    for i in range(1, nh):
        a2a_to(i).wait_recv()
    next_copy.start()
    query_copy = remote(
        fresh.at[0], qpart, part_send.at[0, count], part_recv.at[0, count], partner
    )
    query_copy.start()
    for k in range(count):
        qc[k, 0:rows] = fresh[0, :, k * HD : (k + 1) * HD]
    for slot in range(1, early):
        pass_on(slot)
    own_copy.wait()
    query_copy.wait_recv()
    for k in range(count):
        columns = slice(k * HD, (k + 1) * HD)
        qc[k, rows : 2 * rows] = qpart[:, columns]
        attend(k, 0, rows, fresh[1, :, columns], fresh[2, :, columns], first=True)
        attend(k, rows, rows, own[0, :, columns], own[1, :, columns], first=True)
        for slot in range(early):
            attend_slot(slot, k)

    def step(slot, carry):
        for k in range(count):
            for side in range(2):
                arrived(slot, k, side)
                ring_next(slot + 1, k, side).start()
            attend_slot(slot, k)
        return carry

    if nfull > early:
        lax.fori_loop(early, nfull - 1, step, 0)
        for k in range(count):
            for side in range(2):
                arrived(nfull - 1, k, side)
                ring_far(k, side).start()
            attend_slot(nfull - 1, k)

    def part_copy(k):
        return remote(
            part_out.at[k], part_in.at[k], part_send.at[0, k], part_recv.at[0, k], partner
        )

    def stat_copy(k):
        return remote(
            stat_out.at[k], stat_in.at[k], part_send.at[1, k], part_recv.at[1, k], partner
        )

    def cfg_copy(k):
        return remote(att.at[k], att_other.at[k], cfg_send.at[k], cfg_recv.at[k], other)

    lane = lax.broadcasted_iota(jnp.int32, (rows, HD), 1)
    for k in range(count):
        for side in range(2):
            ring_far(k, side).wait_recv()
        for start in (rows, 0):
            attend(k, start, rows, far[k, 0], far[k, 1])
        part_out[k] = summed[k, rows : 2 * rows].astype(BF16)
        total = jnp.sum(totals[k, rows : 2 * rows], axis=1, keepdims=True)
        stats = jnp.where(lane < HD // 2, maxima[k, rows : 2 * rows], total)
        stat_out[k] = jnp.transpose(stats)[HD // 2 - 8 : HD // 2 + 8]
        part_copy(k).start()
        stat_copy(k).start()

    for k in range(count):
        part_copy(k).wait_recv()
        stat_copy(k).wait_recv()
        max_here = maxima[k, 0:rows]
        total_here = jnp.sum(totals[k, 0:rows], axis=1, keepdims=True)
        max_there = jnp.transpose(jnp.broadcast_to(stat_in[k, 0:1], (HD, rows)))
        total_there = jnp.transpose(jnp.broadcast_to(stat_in[k, 8:9], (HD, rows)))
        top = jnp.maximum(max_here, max_there)
        keep = jnp.exp2((max_here - top) * SCALE2)
        add = jnp.exp2((max_there - top) * SCALE2)
        total = total_here * keep + total_there * add
        value = summed[k, 0:rows] * keep + part_in[k].astype(F32) * add
        att[k] = (value / total).astype(BF16)
        cfg_copy(k).start()

    weight_copy.wait()
    mine = jnp.where(cfg == 0, GUIDE, 1.0 - GUIDE)
    theirs = jnp.where(cfg == 0, 1.0 - GUIDE, GUIDE)
    for k in range(count):
        cfg_copy(k).wait_recv()
        mixed[:, k * HD : (k + 1) * HD] = (
            mine * att[k].astype(F32) + theirs * att_other[k].astype(F32)
        ).astype(BF16)

    piece = 512 if half % 512 == 0 else half

    def project(j, carry):
        columns = pl.ds(pl.multiple_of(j * piece, HD), piece)
        block = jnp.dot(mixed[...], weight[:, columns], preferred_element_type=F32)
        rs_out[:, :, columns] = block.astype(BF16).reshape(nh, tok, piece)
        return carry

    lax.fori_loop(0, half // piece, project, 0)

    def rs_copy(i):
        return remote(
            rs_out.at[lax.rem(head + i, nh)],
            rs_in.at[i],
            rs_send.at[i],
            rs_recv.at[i],
            peers[i - 1],
        )

    for i in range(1, nh):
        rs_copy(i).start()
    tokens_copy.wait()
    gate_copy.wait()
    for i in range(1, nh):
        rs_copy(i).wait_recv()

    def finish(j, carry):
        columns = pl.ds(pl.multiple_of(j * piece, HD), piece)
        value = rs_out[head, :, columns].astype(F32)
        for i in range(1, nh):
            value = value + rs_in[i, :, columns].astype(F32)
        guided_ref[:, columns] = (
            tokens[:, columns].astype(F32) + gate[:, columns] * value
        ).astype(BF16)
        return carry

    lax.fori_loop(0, half // piece, finish, 0)

    next_copy.wait()
    query_copy.wait_send()
    for k in range(count):
        for side in range(2):
            ring_first(k, side).wait_send()
            ring_far(k, side).wait_send()
        part_copy(k).wait_send()
        stat_copy(k).wait_send()
        cfg_copy(k).wait_send()

    def sent(slot, carry):
        for k in range(count):
            for side in range(2):
                ring_next(slot, k, side).wait_send()
        return carry

    lax.fori_loop(1, nfull, sent, 0)
    for i in range(1, nh):
        a2a_to(i).wait_send()
        rs_copy(i).wait_send()


def solution(mesh):
    nz = mesh.shape["patch"] // 2
    nh = mesh.shape["head"]

    def body(qkv, stale_kv, tokens_in, out_weight, gate):
        tok = qkv.shape[2]
        rows = tok * nh
        width = stale_kv.shape[3]
        count = width // HD
        half = tokens_in.shape[1]
        nfull = nz // 2 - 1
        anywhere = pl.BlockSpec(memory_space=pl.ANY)
        dma = pltpu.SemaphoreType.DMA
        return pl.pallas_call(
            functools.partial(kernel, nz, nh),
            out_shape=(
                jax.ShapeDtypeStruct((1, 2, rows, width), BF16),
                jax.ShapeDtypeStruct((tok, half), BF16),
            ),
            in_specs=[anywhere] * 5,
            out_specs=(anywhere, pl.BlockSpec(memory_space=pltpu.VMEM)),
            scratch_shapes=[
                pltpu.VMEM((3, rows, width), BF16),
                pltpu.VMEM((2, rows, width), BF16),
                pltpu.VMEM((nfull, count, 2, 2, rows, HD), BF16),
                pltpu.VMEM((count, 2, rows, HD), BF16),
                pltpu.VMEM((count, 2 * rows, HD), BF16),
                pltpu.VMEM((rows, width), BF16),
                pltpu.VMEM((count, 2 * rows, HD), F32),
                pltpu.VMEM((count, 2 * rows, HD), F32),
                pltpu.VMEM((count, 2 * rows, HD), F32),
                pltpu.VMEM((count, rows, HD), BF16),
                pltpu.VMEM((count, rows, HD), BF16),
                pltpu.VMEM((count, 16, rows), F32),
                pltpu.VMEM((count, 16, rows), F32),
                pltpu.VMEM((count, rows, HD), BF16),
                pltpu.VMEM((count, rows, HD), BF16),
                pltpu.VMEM((rows, width), BF16),
                pltpu.VMEM((width, half), BF16),
                pltpu.VMEM((tok, half), BF16),
                pltpu.VMEM((1, half), F32),
                pltpu.VMEM((nh, tok, half), BF16),
                pltpu.VMEM((nh, tok, half), BF16),
                dma((2, nfull + 1, count)),
                dma((2, nfull + 1, count)),
                dma((nh,)),
                dma((nh,)),
                dma((2, count + 1)),
                dma((2, count + 1)),
                dma((count,)),
                dma((count,)),
                dma((nh,)),
                dma((nh,)),
                dma((6,)),
            ],
            compiler_params=pltpu.CompilerParams(
                collective_id=0, has_side_effects=True, vmem_limit_bytes=40 * 1024 * 1024
            ),
        )(qkv, stale_kv, tokens_in, out_weight, gate.reshape(1, half))

    in_specs = (
        P("cfg", None, ("patch", "head"), None),
        P("cfg", None, "patch", "head"),
        P(("patch", "head"), "cfg"),
        P("head", None),
        P("cfg"),
    )
    out_specs = (P("cfg", None, "patch", "head"), P(("patch", "head"), "cfg"))
    return jax.shard_map(body, mesh=mesh, in_specs=in_specs, out_specs=out_specs, check_vma=False)
```

time: 499 us -> 107 us (0.21)
  waiting for transfers between devices: 320 us -> 0 us
  Pallas kernels: 0 us -> 99.5 us
  local copies, waits for them, and re-layouts: 82.1 us -> 6.71 us
  matrix products: 50.5 us -> 0 us
  other arithmetic: 17.1 us -> 0 us
  between operations: 13.9 us -> 0.64 us
  starting transfers between devices: 11.3 us -> 0 us
    all_gather x2 -> x0, waiting for transfers between devices: 207 us -> none  [the longest x1 115 us: body(): values_piece = lax.all_gather(stale_kv[0, 1], 'patch', axis=0, tiled=True)]
    reduce_scatter x1 -> x0, waiting for transfers between devices: 102 us -> none  [body(): lax.psum_scatter(partial_terms.astype(jnp.bfloat16), 'head', scatter_dime...]
    pallas_call x0 -> x1, Pallas kernels: none -> 99.5 us  [body(): pl.pallas_call(functools.partial(kernel, nz, nh), out_shape=(jax.ShapeDty...]
    dot_general x35 -> x0, matrix products: 50.5 us -> none  [the longest x16 24.6 us: one_block(): jnp.einsum('hqk,khd->hqd', block_weights.astype(jnp.bfloat16), value_bloc...]
    reshape x2 -> x1, local copies, waits for them, and re-layouts: 33.3 us -> 0.7 us  [body(): gate.reshape(1, half)]
    while x19 -> x0, local copies, waits for them, and re-layouts: 15.8 us -> none  [the longest x3 15.7 us: body(): lax.scan(one_block, initial, (keys_blocks, values_blocks, offsets))]
    and x16 -> x0, other arithmetic: 10.4 us -> none  [one_block(): inside = (position >= own_start) & (position < own_start + rows)]
    all_to_all x1 -> x0, waiting for transfers between devices: 9.58 us -> none  [body(): lax.all_to_all(qkv, 'head', split_axis=3, concat_axis=2, tiled=True)]
  transfers between devices with their start and end apart: 5 -> 0, of which waited for: 5 -> 0; matrix products, arithmetic and copies ran while one was open for 10% -> 0% of each run, Pallas kernels for 0% -> 0%
where the time goes in v1:
time: 107 us
  Pallas kernels  99.5 us (93%)
  local copies, waits for them, and re-layouts  6.71 us (6%)
    pallas_call x1, Pallas kernels, body(): pl.pallas_call(functools.partial(kernel, nz, nh), out_shape=(jax.ShapeDty...  99.5 us
    unnamed x10, local copies, waits for them, and re-layouts  6 us

profile of v1, /device:TPU:1, one launch (start us, length us, event | category | flops | bytes accessed | tf_op | source)
XLA Modules:
  0.0 106.9 jit_solution(14760637702081742788)
XLA Ops:
  0.6 0.7 reshape.7.gate_ref
  1.3 0.0 copy-start
  1.3 1.7 %copy-done = bf16[384,3072]{1,0:T(8,128)(2,1)S(1)} copy-done((bf16[384,3072]{1,0:T(8,128)(2,1)S(1)}, bf16[384,3072]{1,0:T(8,128)(2,1)}, u32[]{:S(2)}) %copy-start) | copy-done | bytes 2359320
  3.0 0.0 copy-start.1
  3.0 1.1 copy-done.1
  4.1 0.0 copy-start.2
  4.1 1.0 copy-done.2
  5.1 0.0 copy-start.3
  5.1 0.9 copy-done.3
  6.0 99.5 %shard_map.68 = (bf16[1,2,256,384]{3,2,1,0:T(8,128)(2,1)S(1)}, bf16[32,1536]{1,0:T(8,128)(2,1)S(1)}) custom-call(bf16[1,3,32,3072]{3,2,1,0:T(8,128)(2,1)S(1)} %copy-done.1, bf16[1,2,256,384]{3,2,1,0:T(8,128)(2,1)S(1)} %copy-done.2, bf16[32,1536]{1,0:T(8,128)(2,1)S(1)} %copy-done.3, bf16[384,3072]{1,0:T(8,128)(2,1)S(1)} %copy-done, f32[1,1536]{1,0:T(1,128)S(1)} %reshape.7.gate_ref), custom_call_target="tpu_custom_call" | custom-call | tf_op jit(solution)/shard_map/pallas_call | solution.py:371
  105.5 0.7 copy.9
  106.2 0.6 copy.10
Async XLA Ops:
  1.3 1.7 %copy-start = (bf16[384,3072]{1,0:T(8,128)(2,1)S(1)}, bf16[384,3072]{1,0:T(8,128)(2,1)}, u32[]{:S(2)}) copy-start(bf16[384,3072]{1,0:T(8,128)(2,1)} %weight_ref.1) | copy-start | bytes 7077892
  3.0 1.1 copy-start.1
  4.1 1.0 copy-start.2
  5.1 0.9 copy-start.3

commit v2 on v1

--- a/solution.py
+++ b/solution.py
@@ -13,6 +13,7 @@
 MESH = pl.DeviceIdType.MESH
 BF16 = jnp.bfloat16
 F32 = jnp.float32
+WINDOW = 2
 SCALE2 = HD ** (-0.5) * math.log2(math.e)
 
 
@@ -87,41 +88,45 @@
             device_id_type=MESH,
         )
 
-    def ring_first(k, side):
-        return remote(
-            stale_ref.at[0, :, :, pl.ds(k * HD, HD)],
-            kv.at[0, k, :, side],
-            ring_send.at[side, 0, k],
-            ring_recv.at[side, 0, k],
+    block = 2 * count
+    last = nfull * block
+
+    def ring_own(n, side):
+        k, part = n // 2, n % 2
+        return remote(
+            stale_ref.at[0, part, :, pl.ds(k * HD, HD)],
+            kv.at[k, part, side],
+            ring_send.at[side, n],
+            ring_recv.at[side, n],
             around[side],
         )
 
-    def ring_next(slot, k, side):
-        return remote(
-            kv.at[slot - 1, k, :, side],
-            kv.at[slot, k, :, side],
-            ring_send.at[side, slot, k],
-            ring_recv.at[side, slot, k],
+    def ring_next(u, part, side):
+        return remote(
+            kv.at[u - count, part, side],
+            kv.at[u, part, side],
+            ring_send.at[side, 2 * u + part],
+            ring_recv.at[side, 2 * u + part],
             around[side],
         )
 
     def ring_far(k, side):
         return remote(
-            kv.at[nfull - 1, k, side, side],
+            kv.at[(nfull - 1) * count + k, side, side],
             far.at[k, side],
-            ring_send.at[side, nfull, k],
-            ring_recv.at[side, nfull, k],
+            ring_send.at[side, last + k],
+            ring_recv.at[side, last + k],
             around[side],
         )
 
-    def arrived(slot, k, side):
-        remote(
-            kv.at[slot, k, :, side],
-            kv.at[slot, k, :, side],
-            ring_send.at[side, slot, k],
-            ring_recv.at[side, slot, k],
+    def chunk(n, side):
+        return remote(
+            far.at[0, side],
+            far.at[0, side],
+            ring_send.at[side, n],
+            ring_recv.at[side, n],
             around[side],
-        ).wait_recv()
+        )
 
     def a2a_to(i):
         target = lax.rem(head + i, nh)
@@ -157,20 +162,22 @@
     gate_copy.start()
     pl.semaphore_wait(barrier, len(greeted))
 
-    for k in range(count):
+    for n in range(block):
         for side in range(2):
-            ring_first(k, side).start()
-    for i in range(1, nh):
-        a2a_to(i).start()
-
-    def pass_on(slot):
-        for k in range(count):
+            if n >= WINDOW:
+                chunk(n - WINDOW, side).wait_send()
+            ring_own(n, side).start()
+        if n == min(WINDOW, block) - 1:
+            for i in range(1, nh):
+                a2a_to(i).start()
+
+    def pass_on(u):
+        for part in range(2):
+            n = 2 * u + part
             for side in range(2):
-                arrived(slot, k, side)
-                if isinstance(slot, int) and slot == nfull - 1:
-                    ring_far(k, side).start()
-                else:
-                    ring_next(slot + 1, k, side).start()
+                chunk(n - block, side).wait_recv()
+                chunk(n - WINDOW, side).wait_send()
+                ring_next(u, part, side).start()
 
     def attend(k, start, size, keys, values, first=False):
         span = pl.ds(start, size)
@@ -199,26 +206,34 @@
             totals[k, span] = totals[k, span] * factor + total
             summed[k, span] = summed[k, span] * factor + product
 
-    def attend_slot(slot, k):
-        keys = kv[slot, k, 0].reshape(2 * rows, HD)
-        values = kv[slot, k, 1].reshape(2 * rows, HD)
+    def attend_chunk(v):
+        k = lax.rem(v, count)
+        keys = kv[v, 0].reshape(2 * rows, HD)
+        values = kv[v, 1].reshape(2 * rows, HD)
         for start in (0, rows):
             attend(k, start, rows, keys, values)
 
-    early = min(2, nfull)
-    pass_on(0)
+    def loop(low, high, work):
+        def step(i, carry):
+            work(i)
+            return carry
+
+        lax.fori_loop(low, high, step, 0)
+
+    chunks = nfull * count
+    begin = min(3 * count, chunks)
+    loop(count, min(2 * count, chunks), pass_on)
     mine_copy.wait()
     for i in range(1, nh):
         a2a_to(i).wait_recv()
-    next_copy.start()
     query_copy = remote(
         fresh.at[0], qpart, part_send.at[0, count], part_recv.at[0, count], partner
     )
     query_copy.start()
+    next_copy.start()
     for k in range(count):
         qc[k, 0:rows] = fresh[0, :, k * HD : (k + 1) * HD]
-    for slot in range(1, early):
-        pass_on(slot)
+    loop(min(2 * count, chunks), begin, pass_on)
     own_copy.wait()
     query_copy.wait_recv()
     for k in range(count):
@@ -226,24 +241,29 @@
         qc[k, rows : 2 * rows] = qpart[:, columns]
         attend(k, 0, rows, fresh[1, :, columns], fresh[2, :, columns], first=True)
         attend(k, rows, rows, own[0, :, columns], own[1, :, columns], first=True)
-        for slot in range(early):
-            attend_slot(slot, k)
-
-    def step(slot, carry):
-        for k in range(count):
-            for side in range(2):
-                arrived(slot, k, side)
-                ring_next(slot + 1, k, side).start()
-            attend_slot(slot, k)
-        return carry
-
-    if nfull > early:
-        lax.fori_loop(early, nfull - 1, step, 0)
-        for k in range(count):
-            for side in range(2):
-                arrived(nfull - 1, k, side)
-                ring_far(k, side).start()
-            attend_slot(nfull - 1, k)
+
+    double = max(0, min(chunks - begin, begin - count))
+
+    def catch_up(i):
+        pass_on(begin + i)
+        loop(2 * i, 2 * i + 2, attend_chunk)
+
+    def follow(u):
+        pass_on(u)
+        attend_chunk(u - count)
+
+    loop(0, double, catch_up)
+    loop(begin + double, chunks, follow)
+    done = 2 * double + max(0, chunks - begin - double)
+    loop(done, chunks - count, attend_chunk)
+    for k in range(count):
+        u = chunks - count + k
+        for side in range(2):
+            for part in range(2):
+                chunk(2 * u + part, side).wait_recv()
+            chunk(last + k - WINDOW, side).wait_send()
+            ring_far(k, side).start()
+        attend_chunk(u)
 
     def part_copy(k):
         return remote(
@@ -296,63 +316,50 @@
         ).astype(BF16)
 
     piece = 512 if half % 512 == 0 else half
-
-    def project(j, carry):
-        columns = pl.ds(pl.multiple_of(j * piece, HD), piece)
-        block = jnp.dot(mixed[...], weight[:, columns], preferred_element_type=F32)
-        rs_out[:, :, columns] = block.astype(BF16).reshape(nh, tok, piece)
-        return carry
-
-    lax.fori_loop(0, half // piece, project, 0)
-
-    def rs_copy(i):
-        return remote(
-            rs_out.at[lax.rem(head + i, nh)],
-            rs_in.at[i],
-            rs_send.at[i],
-            rs_recv.at[i],
+    pieces = half // piece
+
+    def rs_copy(i, j):
+        columns = pl.ds(j * piece, piece)
+        return remote(
+            rs_out.at[lax.rem(head + i, nh), :, columns],
+            rs_in.at[i, :, columns],
+            rs_send.at[i, j],
+            rs_recv.at[i, j],
             peers[i - 1],
         )
 
-    for i in range(1, nh):
-        rs_copy(i).start()
+    for j in range(pieces):
+        columns = pl.ds(j * piece, piece)
+        result = jnp.dot(mixed[...], weight[:, columns], preferred_element_type=F32)
+        rs_out[:, :, columns] = result.astype(BF16).reshape(nh, tok, piece)
+        for i in range(1, nh):
+            rs_copy(i, j).start()
     tokens_copy.wait()
     gate_copy.wait()
-    for i in range(1, nh):
-        rs_copy(i).wait_recv()
-
-    def finish(j, carry):
-        columns = pl.ds(pl.multiple_of(j * piece, HD), piece)
+    for j in range(pieces):
+        columns = pl.ds(j * piece, piece)
+        for i in range(1, nh):
+            rs_copy(i, j).wait_recv()
         value = rs_out[head, :, columns].astype(F32)
         for i in range(1, nh):
             value = value + rs_in[i, :, columns].astype(F32)
-        guided_ref[:, columns] = (
-            tokens[:, columns].astype(F32) + gate[:, columns] * value
-        ).astype(BF16)
-        return carry
-
-    lax.fori_loop(0, half // piece, finish, 0)
+        scaled = gate[columns].reshape(1, piece) * value
+        guided_ref[:, columns] = (tokens[:, columns].astype(F32) + scaled).astype(BF16)
 
     next_copy.wait()
     query_copy.wait_send()
-    for k in range(count):
+    for n in range(last + count - WINDOW, last + count):
         for side in range(2):
-            ring_first(k, side).wait_send()
-            ring_far(k, side).wait_send()
+            chunk(n, side).wait_send()
+    for k in range(count):
         part_copy(k).wait_send()
         stat_copy(k).wait_send()
         cfg_copy(k).wait_send()
 
-    def sent(slot, carry):
-        for k in range(count):
-            for side in range(2):
-                ring_next(slot, k, side).wait_send()
-        return carry
-
-    lax.fori_loop(1, nfull, sent, 0)
     for i in range(1, nh):
         a2a_to(i).wait_send()
-        rs_copy(i).wait_send()
+        for j in range(pieces):
+            rs_copy(i, j).wait_send()
 
 
 def solution(mesh):
@@ -366,6 +373,7 @@
         count = width // HD
         half = tokens_in.shape[1]
         nfull = nz // 2 - 1
+        pieces = half // 512 if half % 512 == 0 else 1
         anywhere = pl.BlockSpec(memory_space=pl.ANY)
         dma = pltpu.SemaphoreType.DMA
         return pl.pallas_call(
@@ -379,7 +387,7 @@
             scratch_shapes=[
                 pltpu.VMEM((3, rows, width), BF16),
                 pltpu.VMEM((2, rows, width), BF16),
-                pltpu.VMEM((nfull, count, 2, 2, rows, HD), BF16),
+                pltpu.VMEM((nfull * count, 2, 2, rows, HD), BF16),
                 pltpu.VMEM((count, 2, rows, HD), BF16),
                 pltpu.VMEM((count, 2 * rows, HD), BF16),
                 pltpu.VMEM((rows, width), BF16),
@@ -395,25 +403,25 @@
                 pltpu.VMEM((rows, width), BF16),
                 pltpu.VMEM((width, half), BF16),
                 pltpu.VMEM((tok, half), BF16),
-                pltpu.VMEM((1, half), F32),
+                pltpu.VMEM((half,), F32),
                 pltpu.VMEM((nh, tok, half), BF16),
                 pltpu.VMEM((nh, tok, half), BF16),
-                dma((2, nfull + 1, count)),
-                dma((2, nfull + 1, count)),
+                dma((2, (2 * nfull + 1) * count)),
+                dma((2, (2 * nfull + 1) * count)),
                 dma((nh,)),
                 dma((nh,)),
                 dma((2, count + 1)),
                 dma((2, count + 1)),
                 dma((count,)),
                 dma((count,)),
-                dma((nh,)),
-                dma((nh,)),
+                dma((nh, pieces)),
+                dma((nh, pieces)),
                 dma((6,)),
             ],
             compiler_params=pltpu.CompilerParams(
-                collective_id=0, has_side_effects=True, vmem_limit_bytes=40 * 1024 * 1024
+                collective_id=0, has_side_effects=True, vmem_limit_bytes=62 * 1024 * 1024
             ),
-        )(qkv, stale_kv, tokens_in, out_weight, gate.reshape(1, half))
+        )(qkv, stale_kv, tokens_in, out_weight, gate)
 
     in_specs = (
         P("cfg", None, ("patch", "head"), None),

time: 107 us -> 105 us (0.981)
  local copies, waits for them, and re-layouts: 6.71 us -> 3.32 us
  Pallas kernels: 99.5 us -> 101 us
    unnamed x10 -> x2, local copies, waits for them, and re-layouts: 6 us -> 3.32 us
    pallas_call x1, Pallas kernels: 99.5 us -> 101 us  [body(): pl.pallas_call(functools.partial(kernel, nz, nh), out_shape=(jax.ShapeDty...]
where the time goes in v2:
time: 105 us
  Pallas kernels  101 us (96%)
  local copies, waits for them, and re-layouts  3.32 us (3%)
    pallas_call x1, Pallas kernels, body(): pl.pallas_call(functools.partial(kernel, nz, nh), out_shape=(jax.ShapeDty...  101 us
    unnamed x2, local copies, waits for them, and re-layouts  3.32 us

profile of v2, /device:TPU:1, one launch (start us, length us, event | category | flops | bytes accessed | tf_op | source)
XLA Modules:
  0.0 104.6 jit_solution(9109757369806195509)
XLA Ops:
  0.6 100.6 %shard_map.68 = (bf16[1,2,256,384]{3,2,1,0:T(8,128)(2,1)}, bf16[32,1536]{1,0:T(8,128)(2,1)}) custom-call(bf16[1,3,32,3072]{3,2,1,0:T(8,128)(2,1)} %qkv_ref.1, bf16[1,2,256,384]{3,2,1,0:T(8,128)(2,1)} %stale_ref.1, bf16[32,1536]{1,0:T(8,128)(2,1)} %tokens_ref.1, bf16[384,3072]{1,0:T(8,128)(2,1)} %weight_ref.1, f32[1536]{0:T(1024)} %gate_ref.1), custom_call_target="tpu_custom_call" | custom-call | tf_op jit(solution)/shard_map/pallas_call | solution.py:379
  101.3 1.8 %copy.9 = bf16[1,2,256,384]{3,2,1,0:T(8,128)(2,1)} copy(bf16[1,2,256,384]{3,2,1,0:T(8,128)(2,1)} %get-tuple-element.4) | data formatting | bytes 786432
  103.1 1.5 %copy.10 = bf16[32,1536]{1,0:T(8,128)(2,1)} copy(bf16[32,1536]{1,0:T(8,128)(2,1)} %get-tuple-element.5) | data formatting | bytes 196608

commit v3 on v2

--- a/solution.py
+++ b/solution.py
@@ -13,7 +13,6 @@
 MESH = pl.DeviceIdType.MESH
 BF16 = jnp.bfloat16
 F32 = jnp.float32
-WINDOW = 2
 SCALE2 = HD ** (-0.5) * math.log2(math.e)
 
 
@@ -41,11 +40,11 @@
     stat_out,
     stat_in,
     att,
-    att_other,
-    mixed,
+    tiles,
     weight,
     tokens,
     gate,
+    sums,
     rs_out,
     rs_in,
     ring_send,
@@ -54,8 +53,10 @@
     a2a_recv,
     part_send,
     part_recv,
-    cfg_send,
-    cfg_recv,
+    tile_send,
+    tile_recv,
+    weight_send,
+    weight_recv,
     rs_send,
     rs_recv,
     local_sem,
@@ -65,6 +66,7 @@
     width = stale_ref.shape[3]
     count = width // HD
     half = tokens_ref.shape[1]
+    nx = nh // 2
     nfull = nz // 2 - 1
     patch = lax.axis_index("patch")
     head = lax.axis_index("head")
@@ -74,9 +76,17 @@
     ahead = {"patch": column * nz + lax.rem(z + 1, nz)}
     behind = {"patch": column * nz + lax.rem(z + nz - 1, nz)}
     partner = {"patch": lax.rem(patch + nz, 2 * nz)}
-    other = {"cfg": 1 - cfg}
     around = (ahead, behind)
     peers = [{"head": lax.rem(head + i, nh)} for i in range(1, nh)]
+    x = lax.rem(head, nx)
+    y_hi = head // nx
+    opposite = {"head": (1 - y_hi) * nx + x}
+
+    def x_peer(i):
+        return {"head": y_hi * nx + lax.rem(x + i, nx)}
+
+    def x_cross(i):
+        return {"head": y_hi * nx + lax.rem(x + i, nx), "cfg": 1 - cfg}
 
     def remote(src, dst, send, recv, device):
         return pltpu.make_async_remote_copy(
@@ -138,6 +148,19 @@
             peers[i - 1],
         )
 
+    features = pl.ds(pl.multiple_of(cfg * half, HD), half)
+    part_rows = width // 4
+
+    def weight_to(i, j):
+        span = pl.ds(j * part_rows, part_rows)
+        return remote(
+            weight_ref.at[span, features],
+            weight.at[x, span],
+            weight_send.at[i, j],
+            weight_recv.at[i, j],
+            x_peer(i),
+        )
+
     own_copy = pltpu.make_async_copy(stale_ref.at[0], own, local_sem.at[0])
     mine_copy = pltpu.make_async_copy(
         qkv_ref.at[0, :, :, pl.ds(pl.multiple_of(head * width, HD), width)],
@@ -145,14 +168,14 @@
         local_sem.at[1],
     )
     weight_copy = pltpu.make_async_copy(
-        weight_ref.at[:, pl.ds(pl.multiple_of(cfg * half, HD), half)], weight, local_sem.at[2]
+        weight_ref.at[:, features], weight.at[x], local_sem.at[2]
     )
     tokens_copy = pltpu.make_async_copy(tokens_ref, tokens, local_sem.at[3])
     gate_copy = pltpu.make_async_copy(gate_ref, gate, local_sem.at[4])
     next_copy = pltpu.make_async_copy(fresh.at[pl.ds(1, 2)], next_ref.at[0], local_sem.at[5])
 
     barrier = pltpu.get_barrier_semaphore()
-    greeted = [ahead, behind, partner, other] + peers
+    greeted = [ahead, behind, partner] + peers + [x_cross(i) for i in range(nx)]
     for device in greeted:
         pl.semaphore_signal(barrier, inc=1, device_id=device, device_id_type=MESH)
     own_copy.start()
@@ -164,10 +187,8 @@
 
     for n in range(block):
         for side in range(2):
-            if n >= WINDOW:
-                chunk(n - WINDOW, side).wait_send()
             ring_own(n, side).start()
-        if n == min(WINDOW, block) - 1:
+        if n == block - 1:
             for i in range(1, nh):
                 a2a_to(i).start()
 
@@ -176,7 +197,6 @@
             n = 2 * u + part
             for side in range(2):
                 chunk(n - block, side).wait_recv()
-                chunk(n - WINDOW, side).wait_send()
                 ring_next(u, part, side).start()
 
     def attend(k, start, size, keys, values, first=False):
@@ -231,6 +251,9 @@
     )
     query_copy.start()
     next_copy.start()
+    for j in range(4):
+        for i in range(1, nx):
+            weight_to(i, j).start()
     for k in range(count):
         qc[k, 0:rows] = fresh[0, :, k * HD : (k + 1) * HD]
     loop(min(2 * count, chunks), begin, pass_on)
@@ -261,7 +284,6 @@
         for side in range(2):
             for part in range(2):
                 chunk(2 * u + part, side).wait_recv()
-            chunk(last + k - WINDOW, side).wait_send()
             ring_far(k, side).start()
         attend_chunk(u)
 
@@ -275,24 +297,31 @@
             stat_out.at[k], stat_in.at[k], part_send.at[1, k], part_recv.at[1, k], partner
         )
 
-    def cfg_copy(k):
-        return remote(att.at[k], att_other.at[k], cfg_send.at[k], cfg_recv.at[k], other)
+    crossing = [(1, i) for i in range(nx)] + [(0, i) for i in range(1, nx)]
+
+    def tile_copy(k, flip, i):
+        return remote(
+            att.at[k, :, lax.rem(x + i, nx)],
+            tiles.at[k, cfg, x],
+            tile_send.at[k, flip, i],
+            tile_recv.at[k, flip, i],
+            x_cross(i) if flip else x_peer(i),
+        )
 
     lane = lax.broadcasted_iota(jnp.int32, (rows, HD), 1)
     for k in range(count):
         for side in range(2):
-            ring_far(k, side).wait_recv()
-        for start in (rows, 0):
-            attend(k, start, rows, far[k, 0], far[k, 1])
+            chunk(last + k, side).wait_recv()
+        attend(k, rows, rows, far[k, 0], far[k, 1])
         part_out[k] = summed[k, rows : 2 * rows].astype(BF16)
+        part_copy(k).start()
         total = jnp.sum(totals[k, rows : 2 * rows], axis=1, keepdims=True)
         stats = jnp.where(lane < HD // 2, maxima[k, rows : 2 * rows], total)
         stat_out[k] = jnp.transpose(stats)[HD // 2 - 8 : HD // 2 + 8]
-        part_copy(k).start()
         stat_copy(k).start()
-
-    for k in range(count):
-        part_copy(k).wait_recv()
+        attend(k, 0, rows, far[k, 0], far[k, 1])
+
+    for k in range(count):
         stat_copy(k).wait_recv()
         max_here = maxima[k, 0:rows]
         total_here = jnp.sum(totals[k, 0:rows], axis=1, keepdims=True)
@@ -302,64 +331,72 @@
         keep = jnp.exp2((max_here - top) * SCALE2)
         add = jnp.exp2((max_there - top) * SCALE2)
         total = total_here * keep + total_there * add
+        part_copy(k).wait_recv()
         value = summed[k, 0:rows] * keep + part_in[k].astype(F32) * add
-        att[k] = (value / total).astype(BF16)
-        cfg_copy(k).start()
+        att[k] = (value / total).astype(BF16).reshape(2, nx, tok, HD)
+        for flip, i in crossing:
+            tile_copy(k, flip, i).start()
+        tiles[k, cfg, x] = att[k, :, x]
 
     weight_copy.wait()
-    mine = jnp.where(cfg == 0, GUIDE, 1.0 - GUIDE)
-    theirs = jnp.where(cfg == 0, 1.0 - GUIDE, GUIDE)
-    for k in range(count):
-        cfg_copy(k).wait_recv()
-        mixed[:, k * HD : (k + 1) * HD] = (
-            mine * att[k].astype(F32) + theirs * att_other[k].astype(F32)
-        ).astype(BF16)
-
+    for i in range(1, nx):
+        for j in range(4):
+            weight_to(i, j).wait_recv()
+    tokens_copy.wait()
+    gate_copy.wait()
     piece = 512 if half % 512 == 0 else half
     pieces = half // piece
 
-    def rs_copy(i, j):
+    def rs_copy(j):
         columns = pl.ds(j * piece, piece)
         return remote(
-            rs_out.at[lax.rem(head + i, nh), :, columns],
-            rs_in.at[i, :, columns],
-            rs_send.at[i, j],
-            rs_recv.at[i, j],
-            peers[i - 1],
-        )
-
+            rs_out.at[:, columns], rs_in.at[:, columns], rs_send.at[j], rs_recv.at[j], opposite
+        )
+
+    for k in range(count):
+        for flip, i in crossing:
+            tile_copy(k, flip, i).wait_recv()
+        both = GUIDE * tiles[k, 0].astype(F32) + (1.0 - GUIDE) * tiles[k, 1].astype(F32)
+        both = both.astype(BF16)
+        table = jnp.concatenate([both[i].reshape(2 * tok, HD) for i in range(nx)], axis=1)
+        for j in range(pieces):
+            columns = pl.ds(j * piece, piece)
+            factors = weight[:, k * HD : (k + 1) * HD, columns].reshape(nx * HD, piece)
+            result = jnp.dot(table, factors, preferred_element_type=F32)
+            result = result.reshape(2, tok, piece)
+            if k == 0:
+                sums[:, :, columns] = result
+            else:
+                sums[:, :, columns] += result
+            if k == count - 1:
+                rs_out[:, columns] = sums[1 - y_hi, :, columns].astype(BF16)
+                rs_copy(j).start()
+    next_copy.wait()
+    query_copy.wait_send()
+
+    def sent(n):
+        for side in range(2):
+            chunk(n, side).wait_send()
+
+    loop(0, last + count, sent)
+    for k in range(count):
+        part_copy(k).wait_send()
+        stat_copy(k).wait_send()
+        for flip, i in crossing:
+            tile_copy(k, flip, i).wait_send()
+    for i in range(1, nh):
+        a2a_to(i).wait_send()
+    for i in range(1, nx):
+        for j in range(4):
+            weight_to(i, j).wait_send()
     for j in range(pieces):
         columns = pl.ds(j * piece, piece)
-        result = jnp.dot(mixed[...], weight[:, columns], preferred_element_type=F32)
-        rs_out[:, :, columns] = result.astype(BF16).reshape(nh, tok, piece)
-        for i in range(1, nh):
-            rs_copy(i, j).start()
-    tokens_copy.wait()
-    gate_copy.wait()
-    for j in range(pieces):
-        columns = pl.ds(j * piece, piece)
-        for i in range(1, nh):
-            rs_copy(i, j).wait_recv()
-        value = rs_out[head, :, columns].astype(F32)
-        for i in range(1, nh):
-            value = value + rs_in[i, :, columns].astype(F32)
+        rs_copy(j).wait_recv()
+        value = sums[y_hi, :, columns] + rs_in[:, columns].astype(F32)
         scaled = gate[columns].reshape(1, piece) * value
         guided_ref[:, columns] = (tokens[:, columns].astype(F32) + scaled).astype(BF16)
-
-    next_copy.wait()
-    query_copy.wait_send()
-    for n in range(last + count - WINDOW, last + count):
-        for side in range(2):
-            chunk(n, side).wait_send()
-    for k in range(count):
-        part_copy(k).wait_send()
-        stat_copy(k).wait_send()
-        cfg_copy(k).wait_send()
-
-    for i in range(1, nh):
-        a2a_to(i).wait_send()
-        for j in range(pieces):
-            rs_copy(i, j).wait_send()
+    for j in range(pieces):
+        rs_copy(j).wait_send()
 
 
 def solution(mesh):
@@ -372,6 +409,7 @@
         width = stale_kv.shape[3]
         count = width // HD
         half = tokens_in.shape[1]
+        nx = nh // 2
         nfull = nz // 2 - 1
         pieces = half // 512 if half % 512 == 0 else 1
         anywhere = pl.BlockSpec(memory_space=pl.ANY)
@@ -398,24 +436,26 @@
                 pltpu.VMEM((count, rows, HD), BF16),
                 pltpu.VMEM((count, 16, rows), F32),
                 pltpu.VMEM((count, 16, rows), F32),
-                pltpu.VMEM((count, rows, HD), BF16),
-                pltpu.VMEM((count, rows, HD), BF16),
-                pltpu.VMEM((rows, width), BF16),
-                pltpu.VMEM((width, half), BF16),
+                pltpu.VMEM((count, 2, nx, tok, HD), BF16),
+                pltpu.VMEM((count, 2, nx, 2, tok, HD), BF16),
+                pltpu.VMEM((nx, width, half), BF16),
                 pltpu.VMEM((tok, half), BF16),
                 pltpu.VMEM((half,), F32),
-                pltpu.VMEM((nh, tok, half), BF16),
-                pltpu.VMEM((nh, tok, half), BF16),
+                pltpu.VMEM((2, tok, half), F32),
+                pltpu.VMEM((tok, half), BF16),
+                pltpu.VMEM((tok, half), BF16),
                 dma((2, (2 * nfull + 1) * count)),
                 dma((2, (2 * nfull + 1) * count)),
                 dma((nh,)),
                 dma((nh,)),
                 dma((2, count + 1)),
                 dma((2, count + 1)),
-                dma((count,)),
-                dma((count,)),
-                dma((nh, pieces)),
-                dma((nh, pieces)),
+                dma((count, 2, nx)),
+                dma((count, 2, nx)),
+                dma((nx, 4)),
+                dma((nx, 4)),
+                dma((pieces,)),
+                dma((pieces,)),
                 dma((6,)),
             ],
             compiler_params=pltpu.CompilerParams(

time: 105 us -> 99.6 us (0.949)
  Pallas kernels: 101 us -> 95.5 us
    pallas_call x1, Pallas kernels: 101 us -> 95.5 us  [body(): pl.pallas_call(functools.partial(kernel, nz, nh), out_shape=(jax.ShapeDty...]
where the time goes in v3:
time: 99.6 us; the launch traced here: 99.4 us
  Pallas kernels  95.5 us (96%)
  local copies, waits for them, and re-layouts  3.32 us (3%)
    pallas_call x1, Pallas kernels, body(): pl.pallas_call(functools.partial(kernel, nz, nh), out_shape=(jax.ShapeDty...  95.5 us
    unnamed x2, local copies, waits for them, and re-layouts  3.32 us

profile of v3, /device:TPU:1, one launch (start us, length us, event | category | flops | bytes accessed | tf_op | source)
XLA Modules:
  0.0 99.4 jit_solution(8087494488443470401)
XLA Ops:
  0.6 95.5 %shard_map.68 = (bf16[1,2,256,384]{3,2,1,0:T(8,128)(2,1)}, bf16[32,1536]{1,0:T(8,128)(2,1)}) custom-call(bf16[1,3,32,3072]{3,2,1,0:T(8,128)(2,1)} %qkv_ref.1, bf16[1,2,256,384]{3,2,1,0:T(8,128)(2,1)} %stale_ref.1, bf16[32,1536]{1,0:T(8,128)(2,1)} %tokens_ref.1, bf16[384,3072]{1,0:T(8,128)(2,1)} %weight_ref.1, f32[1536]{0:T(1024)} %gate_ref.1), custom_call_target="tpu_custom_call" | custom-call | tf_op jit(solution)/shard_map/pallas_call | solution.py:417
  96.1 1.8 %copy.9 = bf16[1,2,256,384]{3,2,1,0:T(8,128)(2,1)} copy(bf16[1,2,256,384]{3,2,1,0:T(8,128)(2,1)} %get-tuple-element.4) | data formatting | bytes 786432
  97.9 1.5 %copy.10 = bf16[32,1536]{1,0:T(8,128)(2,1)} copy(bf16[32,1536]{1,0:T(8,128)(2,1)} %get-tuple-element.5) | data formatting | bytes 196608

commit v4 on v3

--- a/solution.py
+++ b/solution.py
@@ -98,45 +98,24 @@
             device_id_type=MESH,
         )
 
-    block = 2 * count
-    last = nfull * block
-
-    def ring_own(n, side):
-        k, part = n // 2, n % 2
-        return remote(
-            stale_ref.at[0, part, :, pl.ds(k * HD, HD)],
-            kv.at[k, part, side],
-            ring_send.at[side, n],
-            ring_recv.at[side, n],
-            around[side],
-        )
-
-    def ring_next(u, part, side):
-        return remote(
-            kv.at[u - count, part, side],
-            kv.at[u, part, side],
-            ring_send.at[side, 2 * u + part],
-            ring_recv.at[side, 2 * u + part],
-            around[side],
-        )
+    last = nfull * count
+
+    def ring(src, dst, n, side):
+        return remote(src, dst, ring_send.at[side, n], ring_recv.at[side, n], around[side])
+
+    def ring_own(k, side):
+        return ring(
+            stale_ref.at[0, :, :, pl.ds(k * HD, HD)], kv.at[k, :, side], k, side
+        )
+
+    def ring_next(u, side):
+        return ring(kv.at[u - count, :, side], kv.at[u, :, side], u, side)
 
     def ring_far(k, side):
-        return remote(
-            kv.at[(nfull - 1) * count + k, side, side],
-            far.at[k, side],
-            ring_send.at[side, last + k],
-            ring_recv.at[side, last + k],
-            around[side],
-        )
+        return ring(kv.at[last - count + k, side, side], far.at[k, side], last + k, side)
 
     def chunk(n, side):
-        return remote(
-            far.at[0, side],
-            far.at[0, side],
-            ring_send.at[side, n],
-            ring_recv.at[side, n],
-            around[side],
-        )
+        return ring(kv.at[0, :, side], kv.at[0, :, side], n, side)
 
     def a2a_to(i):
         target = lax.rem(head + i, nh)
@@ -185,19 +164,16 @@
     gate_copy.start()
     pl.semaphore_wait(barrier, len(greeted))
 
-    for n in range(block):
-        for side in range(2):
-            ring_own(n, side).start()
-        if n == block - 1:
-            for i in range(1, nh):
-                a2a_to(i).start()
+    for k in range(count):
+        for side in range(2):
+            ring_own(k, side).start()
+    for i in range(1, nh):
+        a2a_to(i).start()
 
     def pass_on(u):
-        for part in range(2):
-            n = 2 * u + part
-            for side in range(2):
-                chunk(n - block, side).wait_recv()
-                ring_next(u, part, side).start()
+        for side in range(2):
+            chunk(u - count, side).wait_recv()
+            ring_next(u, side).start()
 
     def attend(k, start, size, keys, values, first=False):
         span = pl.ds(start, size)
@@ -282,8 +258,7 @@
     for k in range(count):
         u = chunks - count + k
         for side in range(2):
-            for part in range(2):
-                chunk(2 * u + part, side).wait_recv()
+            chunk(u, side).wait_recv()
             ring_far(k, side).start()
         attend_chunk(u)
 
@@ -311,7 +286,7 @@
     lane = lax.broadcasted_iota(jnp.int32, (rows, HD), 1)
     for k in range(count):
         for side in range(2):
-            chunk(last + k, side).wait_recv()
+            ring_far(k, side).wait_recv()
         attend(k, rows, rows, far[k, 0], far[k, 1])
         part_out[k] = summed[k, rows : 2 * rows].astype(BF16)
         part_copy(k).start()
@@ -378,8 +353,10 @@
         for side in range(2):
             chunk(n, side).wait_send()
 
-    loop(0, last + count, sent)
-    for k in range(count):
+    loop(0, last, sent)
+    for k in range(count):
+        for side in range(2):
+            ring_far(k, side).wait_send()
         part_copy(k).wait_send()
         stat_copy(k).wait_send()
         for flip, i in crossing:
@@ -417,11 +394,11 @@
         return pl.pallas_call(
             functools.partial(kernel, nz, nh),
             out_shape=(
-                jax.ShapeDtypeStruct((1, 2, rows, width), BF16),
-                jax.ShapeDtypeStruct((tok, half), BF16),
+                pltpu.VMEM((1, 2, rows, width), BF16),
+                pltpu.VMEM((tok, half), BF16),
             ),
             in_specs=[anywhere] * 5,
-            out_specs=(anywhere, pl.BlockSpec(memory_space=pltpu.VMEM)),
+            out_specs=(pl.BlockSpec(memory_space=pltpu.VMEM),) * 2,
             scratch_shapes=[
                 pltpu.VMEM((3, rows, width), BF16),
                 pltpu.VMEM((2, rows, width), BF16),
@@ -444,8 +421,8 @@
                 pltpu.VMEM((2, tok, half), F32),
                 pltpu.VMEM((tok, half), BF16),
                 pltpu.VMEM((tok, half), BF16),
-                dma((2, (2 * nfull + 1) * count)),
-                dma((2, (2 * nfull + 1) * count)),
+                dma((2, (nfull + 1) * count)),
+                dma((2, (nfull + 1) * count)),
                 dma((nh,)),
                 dma((nh,)),
                 dma((2, count + 1)),

time: 99.6 us -> 96.2 us (0.966)
  local copies, waits for them, and re-layouts: 3.32 us -> 1.39 us
  Pallas kernels: 95.5 us -> 94.1 us
    unnamed x2, local copies, waits for them, and re-layouts: 3.32 us -> 1.39 us
    pallas_call x1, Pallas kernels: 95.5 us -> 94.1 us  [body(): pl.pallas_call(functools.partial(kernel, nz, nh), out_shape=(pltpu.VMEM((...]
where the time goes in v4:
time: 96.2 us; the launch traced here: 96.1 us
  Pallas kernels  94.1 us (98%)
  local copies, waits for them, and re-layouts  1.39 us (1%)
    pallas_call x1, Pallas kernels, body(): pl.pallas_call(functools.partial(kernel, nz, nh), out_shape=(pltpu.VMEM((...  94.1 us

profile of v4, /device:TPU:1, one launch (start us, length us, event | category | flops | bytes accessed | tf_op | source)
XLA Modules:
  0.0 96.1 jit_solution(18172723270686150099)
XLA Ops:
  0.6 94.1 %shard_map.68 = (bf16[1,2,256,384]{3,2,1,0:T(8,128)(2,1)S(1)}, bf16[32,1536]{1,0:T(8,128)(2,1)S(1)}) custom-call(bf16[1,3,32,3072]{3,2,1,0:T(8,128)(2,1)} %qkv_ref.1, bf16[1,2,256,384]{3,2,1,0:T(8,128)(2,1)} %stale_ref.1, bf16[32,1536]{1,0:T(8,128)(2,1)} %tokens_ref.1, bf16[384,3072]{1,0:T(8,128)(2,1)} %weight_ref.1, f32[1536]{0:T(1024)} %gate_ref.1), custom_call_target="tpu_custom_call" | custom-call | tf_op jit(solution)/shard_map/pallas_call | solution.py:394
  94.7 0.7 copy.9
  95.5 0.6 copy.10

commit v5 on v4

--- a/solution.py
+++ b/solution.py
@@ -288,20 +288,20 @@
         for side in range(2):
             ring_far(k, side).wait_recv()
         attend(k, rows, rows, far[k, 0], far[k, 1])
+        total = jnp.sum(totals[k, rows : 2 * rows], axis=1, keepdims=True)
+        stats = jnp.where(lane < 4, maxima[k, rows : 2 * rows], total)
+        stat_out[k] = jnp.transpose(stats)[0:8]
+        stat_copy(k).start()
         part_out[k] = summed[k, rows : 2 * rows].astype(BF16)
         part_copy(k).start()
-        total = jnp.sum(totals[k, rows : 2 * rows], axis=1, keepdims=True)
-        stats = jnp.where(lane < HD // 2, maxima[k, rows : 2 * rows], total)
-        stat_out[k] = jnp.transpose(stats)[HD // 2 - 8 : HD // 2 + 8]
-        stat_copy(k).start()
         attend(k, 0, rows, far[k, 0], far[k, 1])
 
     for k in range(count):
-        stat_copy(k).wait_recv()
         max_here = maxima[k, 0:rows]
         total_here = jnp.sum(totals[k, 0:rows], axis=1, keepdims=True)
+        stat_copy(k).wait_recv()
         max_there = jnp.transpose(jnp.broadcast_to(stat_in[k, 0:1], (HD, rows)))
-        total_there = jnp.transpose(jnp.broadcast_to(stat_in[k, 8:9], (HD, rows)))
+        total_there = jnp.transpose(jnp.broadcast_to(stat_in[k, 4:5], (HD, rows)))
         top = jnp.maximum(max_here, max_there)
         keep = jnp.exp2((max_here - top) * SCALE2)
         add = jnp.exp2((max_there - top) * SCALE2)
@@ -411,8 +411,8 @@
                 pltpu.VMEM((count, 2 * rows, HD), F32),
                 pltpu.VMEM((count, rows, HD), BF16),
                 pltpu.VMEM((count, rows, HD), BF16),
-                pltpu.VMEM((count, 16, rows), F32),
-                pltpu.VMEM((count, 16, rows), F32),
+                pltpu.VMEM((count, 8, rows), F32),
+                pltpu.VMEM((count, 8, rows), F32),
                 pltpu.VMEM((count, 2, nx, tok, HD), BF16),
                 pltpu.VMEM((count, 2, nx, 2, tok, HD), BF16),
                 pltpu.VMEM((nx, width, half), BF16),

time: 96.2 us -> 95.7 us (level)
  no operation moved by 1% of the time
where the time goes in v5:
time: 95.7 us; the launch traced here: 95.6 us
  Pallas kernels  93.5 us (98%)
  local copies, waits for them, and re-layouts  1.39 us (1%)
    pallas_call x1, Pallas kernels, body(): pl.pallas_call(functools.partial(kernel, nz, nh), out_shape=(pltpu.VMEM((...  93.5 us

profile of v5, /device:TPU:1, one launch (start us, length us, event | category | flops | bytes accessed | tf_op | source)
XLA Modules:
  0.0 95.6 jit_solution(16321153397633468996)
XLA Ops:
  0.6 93.5 %shard_map.68 = (bf16[1,2,256,384]{3,2,1,0:T(8,128)(2,1)S(1)}, bf16[32,1536]{1,0:T(8,128)(2,1)S(1)}) custom-call(bf16[1,3,32,3072]{3,2,1,0:T(8,128)(2,1)} %qkv_ref.1, bf16[1,2,256,384]{3,2,1,0:T(8,128)(2,1)} %stale_ref.1, bf16[32,1536]{1,0:T(8,128)(2,1)} %tokens_ref.1, bf16[384,3072]{1,0:T(8,128)(2,1)} %weight_ref.1, f32[1536]{0:T(1024)} %gate_ref.1), custom_call_target="tpu_custom_call" | custom-call | tf_op jit(solution)/shard_map/pallas_call | solution.py:394
  94.2 0.7 copy.9
  94.9 0.6 copy.10

commit v6 on v5

--- a/solution.py
+++ b/solution.py
@@ -111,8 +111,10 @@
     def ring_next(u, side):
         return ring(kv.at[u - count, :, side], kv.at[u, :, side], u, side)
 
-    def ring_far(k, side):
-        return ring(kv.at[last - count + k, side, side], far.at[k, side], last + k, side)
+    def ring_far(k, part):
+        side = 1 if part == 1 or k == 0 else 0
+        n = last + 2 * k + part
+        return ring(kv.at[last - count + k, part, side], far.at[k, part], n, side)
 
     def chunk(n, side):
         return ring(kv.at[0, :, side], kv.at[0, :, side], n, side)
@@ -259,7 +261,8 @@
         u = chunks - count + k
         for side in range(2):
             chunk(u, side).wait_recv()
-            ring_far(k, side).start()
+        for part in range(2):
+            ring_far(k, part).start()
         attend_chunk(u)
 
     def part_copy(k):
@@ -421,8 +424,8 @@
                 pltpu.VMEM((2, tok, half), F32),
                 pltpu.VMEM((tok, half), BF16),
                 pltpu.VMEM((tok, half), BF16),
-                dma((2, (nfull + 1) * count)),
-                dma((2, (nfull + 1) * count)),
+                dma((2, (nfull + 2) * count)),
+                dma((2, (nfull + 2) * count)),
                 dma((nh,)),
                 dma((nh,)),
                 dma((2, count + 1)),

time: 95.7 us -> 95.7 us (level)
  no operation moved by 1% of the time
where the time goes in v6:
time: 95.7 us; the launch traced here: 95.5 us
  Pallas kernels  93.5 us (98%)
  local copies, waits for them, and re-layouts  1.39 us (1%)
    pallas_call x1, Pallas kernels, body(): pl.pallas_call(functools.partial(kernel, nz, nh), out_shape=(pltpu.VMEM((...  93.5 us

profile of v6, /device:TPU:1, one launch (start us, length us, event | category | flops | bytes accessed | tf_op | source)
XLA Modules:
  0.0 95.5 jit_solution(18285288987149208523)
XLA Ops:
  0.6 93.5 %shard_map.68 = (bf16[1,2,256,384]{3,2,1,0:T(8,128)(2,1)S(1)}, bf16[32,1536]{1,0:T(8,128)(2,1)S(1)}) custom-call(bf16[1,3,32,3072]{3,2,1,0:T(8,128)(2,1)} %qkv_ref.1, bf16[1,2,256,384]{3,2,1,0:T(8,128)(2,1)} %stale_ref.1, bf16[32,1536]{1,0:T(8,128)(2,1)} %tokens_ref.1, bf16[384,3072]{1,0:T(8,128)(2,1)} %weight_ref.1, f32[1536]{0:T(1024)} %gate_ref.1), custom_call_target="tpu_custom_call" | custom-call | tf_op jit(solution)/shard_map/pallas_call | solution.py:397
  94.2 0.7 copy.9
  94.9 0.6 copy.10
